TPU v7x, 256 devices: a whole 4x4x8 slice. The times are simulated.
256 devices in a mesh: dp: 4 (over y_lo, core), expert: 8 (over z), tensor: 8 (over x, y_hi).
Axes of the slice: x: 4, y: 4 (y_hi: 2, y_lo: 2; y = y_hi * 2 + y_lo), z: 8, core: 2. Of those that a mesh axis runs over, the one named last changes fastest.
Arguments:
- grad_out: bfloat16 [32768, 2048], P(('dp', 'expert', 'tensor')), may hold values from -6 to 6
- expert_ids: int32 [32768, 2], P(('dp', 'expert', 'tensor')), may hold values from 0 to 63, all different within a row; in each aligned block of 128 rows (0 to 127, 128 to 255, ...) at most 5 rows name the same one
- gate_weights: float32 [32768, 2], P(('dp', 'expert', 'tensor')), may hold values from 0.05 to 0.6
- overflow: int32 [32768, 2], P(('dp', 'expert', 'tensor')), may hold values 0 or 1
- saved_gate: bfloat16 [64, 4, 64, 5, 1408], P(('expert', 'tensor'), None, None, None, 'dp'), may hold values from -6 to 6
- saved_up: bfloat16 [64, 4, 64, 5, 1408], P(('expert', 'tensor'), None, None, None, 'dp'), may hold values from -6 to 6
- w_gate: bfloat16 [64, 2048, 1408], P(('expert', 'tensor'), None, 'dp'), may hold values from -0.125 to 0.125
- w_up: bfloat16 [64, 2048, 1408], P(('expert', 'tensor'), None, 'dp'), may hold values from -0.125 to 0.125
- w_down: bfloat16 [64, 1408, 2048], P(('expert', 'tensor'), 'dp'), may hold values from -0.15625 to 0.15625
- shared_gate_act: bfloat16 [32768, 1408], P(('dp', 'expert'), 'tensor'), may hold values from -6 to 6
- shared_up_act: bfloat16 [32768, 1408], P(('dp', 'expert'), 'tensor'), may hold values from -6 to 6
- ws_gate: bfloat16 [2048, 1408], P(None, 'tensor'), may hold values from -0.125 to 0.125
- ws_up: bfloat16 [2048, 1408], P(None, 'tensor'), may hold values from -0.125 to 0.125
- ws_down: bfloat16 [1408, 2048], P('tensor'), may hold values from -0.15625 to 0.15625
- w_out: bfloat16 [2048, 2048], P('tensor'), may hold values from -0.125 to 0.125
Outputs:
- grad_hidden: bfloat16 [32768, 2048], P(('dp', 'expert', 'tensor'))
- grad_context: bfloat16 [32768, 2048], P(('dp', 'expert'), 'tensor')
Inputs may be any that keep to these rules, and one draw needn't show every extreme that they name: `expert_ids`: each row names 2 different experts; within the rows of one device (aligned blocks of 128 rows) no expert is named by more than 5 rows, a bound that some block reaches.
All inputs are finite; a program needn't handle non-finite values. No bound on the sum of `overflow` on one device may be relied on, other than what follows from the above.
Results may differ from a plain program's by a relative error of at most 0.015.
Values may be sent and summed in bfloat16 or wider, within the bound.
A program may use at most 128 MiB of HBM per device.

v0:
```python
import jax
import jax.numpy as jnp
from jax import lax
from jax.sharding import PartitionSpec as P


def rank_in_block(pair_experts, expert_total):
    onehot = (pair_experts[:, None] == jnp.arange(expert_total, dtype=jnp.int32)[None, :]).astype(
        jnp.int32
    )
    earlier = jnp.cumsum(onehot, axis=0) - onehot
    return jnp.sum(earlier * onehot, axis=1)


def fill_slots(pair_grads, pair_experts, expert_total, capacity):
    pair_count, model_width = pair_grads.shape
    destination = pair_experts * capacity + rank_in_block(pair_experts, expert_total)
    source = jnp.full((expert_total * capacity,), pair_count, jnp.int32)
    source = source.at[destination].set(jnp.arange(pair_count, dtype=jnp.int32))
    padded = jnp.concatenate([pair_grads, jnp.zeros((1, model_width), pair_grads.dtype)], axis=0)
    return (padded[source].reshape(expert_total, capacity, model_width), destination)


def weighted_pairs(grads, weights):
    scaled = grads.astype(jnp.float32)[:, None, :] * weights.astype(jnp.float32)[:, :, None]
    return scaled.astype(jnp.bfloat16).reshape(-1, grads.shape[1])


def swiglu_backward(hidden_activation, gate_act, up_act):
    gate_value = gate_act.astype(jnp.float32)
    sigmoid_value = jax.nn.sigmoid(gate_value)
    gate_input_gradient = (
        hidden_activation
        * up_act.astype(jnp.float32)
        * sigmoid_value
        * (1.0 + gate_value * (1.0 - sigmoid_value))
    ).astype(jnp.bfloat16)
    up_input_gradient = (hidden_activation * gate_value * sigmoid_value).astype(jnp.bfloat16)
    return (gate_input_gradient, up_input_gradient)


def expert_terms(
    capacity_slot_rows,
    gate_act,
    up_act,
    gate_projection_weight,
    up_projection_weight,
    down_projection_weight,
):
    hidden_activation = jnp.einsum(
        "cyg,cog->cyo",
        capacity_slot_rows,
        down_projection_weight,
        preferred_element_type=jnp.float32,
    )
    gate_input_gradient, up_input_gradient = swiglu_backward(hidden_activation, gate_act, up_act)
    input_gradient_output = jnp.einsum(
        "etv,ebv->etb",
        gate_input_gradient,
        gate_projection_weight,
        preferred_element_type=jnp.float32,
    )
    input_gradient_output = input_gradient_output + jnp.einsum(
        "etv,ebv->etb", up_input_gradient, up_projection_weight, preferred_element_type=jnp.float32
    )
    return lax.optimization_barrier(input_gradient_output.astype(jnp.bfloat16))


def body(
    grad_out,
    expert_ids,
    gate_weights,
    overflow,
    saved_gate,
    saved_up,
    w_gate,
    w_up,
    w_down,
    shared_gate_act,
    shared_up_act,
    ws_gate,
    ws_up,
    ws_down,
    w_out,
):
    dp_count = lax.axis_size("dp")
    group_count = lax.axis_size(("expert", "tensor"))
    expert_local, unused_dp, unused_group, capacity, unit_part = saved_gate.shape
    expert_total = expert_local * group_count
    token_count, model_width = grad_out.shape
    top_count = expert_ids.shape[1]
    flag_values = overflow.astype(jnp.float32)
    routed_weight = (gate_weights * (1.0 - flag_values)).astype(jnp.bfloat16)
    shared_weight = 1.0 + jnp.sum(gate_weights * flag_values, axis=1)
    pair_grads = weighted_pairs(grad_out, routed_weight)
    filled, destination = fill_slots(pair_grads, expert_ids.reshape(-1), expert_total, capacity)
    arrived = lax.all_to_all(
        filled[:, None], ("expert", "tensor"), split_axis=0, concat_axis=1, tiled=True
    )
    everyone = lax.all_gather(arrived[:, None], "dp", axis=1, tiled=True)
    terms = expert_terms(
        everyone.reshape(expert_local, -1, model_width),
        saved_gate.reshape(expert_local, -1, unit_part),
        saved_up.reshape(expert_local, -1, unit_part),
        w_gate,
        w_up,
        w_down,
    )
    terms = terms.astype(jnp.float32).reshape(
        expert_local, dp_count, group_count, capacity, model_width
    )
    summed = lax.psum_scatter(
        terms.astype(jnp.bfloat16), "dp", scatter_dimension=1, tiled=True
    ).astype(jnp.float32)
    returned = lax.all_to_all(
        summed[:, 0].astype(jnp.bfloat16),
        ("expert", "tensor"),
        split_axis=1,
        concat_axis=0,
        tiled=True,
    ).astype(jnp.float32)
    picked = returned.reshape(expert_total * capacity, model_width)[destination]
    routed = jnp.sum(picked.reshape(token_count, top_count, model_width), axis=1)
    routed_total = routed.astype(jnp.bfloat16)
    shared_grad = (grad_out.astype(jnp.float32) * shared_weight[:, None]).astype(jnp.bfloat16)
    group_shared = lax.all_gather(shared_grad, "tensor", axis=0, tiled=True)
    shared_hidden = jnp.einsum(
        "td,fd->tf", group_shared, ws_down, preferred_element_type=jnp.float32
    )
    shared_gate_grad, shared_up_grad = swiglu_backward(
        shared_hidden, shared_gate_act, shared_up_act
    )
    partial_value = jnp.einsum(
        "tf,df->td", shared_gate_grad, ws_gate, preferred_element_type=jnp.float32
    )
    partial_value = partial_value + jnp.einsum(
        "tf,df->td", shared_up_grad, ws_up, preferred_element_type=jnp.float32
    )
    partial_value = lax.optimization_barrier(partial_value.astype(jnp.bfloat16)).astype(jnp.float32)
    shared_total = lax.psum(partial_value.astype(jnp.bfloat16), "tensor").astype(jnp.float32)
    group_grads, group_routed = (
        lax.all_gather(grad_out, "tensor", axis=0, tiled=True),
        lax.all_gather(routed_total, "tensor", axis=0, tiled=True),
    )
    grad_group = (
        group_grads.astype(jnp.float32) + shared_total + group_routed.astype(jnp.float32)
    ).astype(jnp.bfloat16)
    position = lax.axis_index("tensor") * token_count
    grad_hidden = lax.dynamic_slice_in_dim(grad_group, position, token_count, 0)
    grad_context = jnp.einsum(
        "td,hd->th", grad_group, w_out, preferred_element_type=jnp.float32
    ).astype(jnp.bfloat16)
    return (grad_hidden, grad_context)


def solution(mesh):
    in_specs = (
        P(("dp", "expert", "tensor"), None),
        P(("dp", "expert", "tensor"), None),
        P(("dp", "expert", "tensor"), None),
        P(("dp", "expert", "tensor"), None),
        P(("expert", "tensor"), None, None, None, "dp"),
        P(("expert", "tensor"), None, None, None, "dp"),
        P(("expert", "tensor"), None, "dp"),
        P(("expert", "tensor"), None, "dp"),
        P(("expert", "tensor"), "dp", None),
        P(("dp", "expert"), "tensor"),
        P(("dp", "expert"), "tensor"),
        P(None, "tensor"),
        P(None, "tensor"),
        P("tensor", None),
        P("tensor", None),
    )
    out_specs = (P(("dp", "expert", "tensor"), None), P(("dp", "expert"), "tensor"))
    return jax.shard_map(body, mesh=mesh, in_specs=in_specs, out_specs=out_specs, check_vma=False)
```

profile of v0, /device:TPU:1, one launch (start us, length us, event | category | flops | bytes accessed | tf_op | source)
XLA Modules:
  0.0 691.3 jit_solution(10206642360038884631)
XLA Ops:
  19.2 3.0 gather_fusion
  24.6 63.7 %all_to_all.8 = bf16[64,1,5,2048]{3,2,1,0:T(8,128)(2,1)S(1)} all-to-all(bf16[64,1,5,2048]{3,2,1,0:T(8,128)(2,1)S(1)} %bitcast.47), channel_id=1, replica_groups=mesh['dp'=4,'expert'=8,'tensor'=8] {'expert','tensor'}, dimensions={0} | all-to-all | bytes 2621440 | tf_op jit(solution)/shard_map/all_to_all | solution.py:97
  93.7 3.6 reshape.159
  99.2 3.5 copy.38
  102.7 3.7 reshape.158
  106.4 2.8 copy.39
  109.2 38.2 %all-gather.12.cloned.1.call-done = bf16[256,1,5,2048]{3,0,2,1:T(8,128)(2,1)} async-done(((bf16[64,1,5,2048]{3,0,2,1:T(8,128)(2,1)}), bf16[256,1,5,2048]{3,0,2,1:T(8,128)(2,1)}) %all-gather.12.cloned.1.call-update) | async-done | bytes 5242896 | tf_op jit(solution)/shard_map/all_gather | solution.py:100
  147.4 8.9 %copy.37 = bf16[256,1,5,2048]{3,2,0,1:T(8,128)(2,1)} copy(bf16[256,1,5,2048]{3,0,2,1:T(8,128)(2,1)} %all-gather.12.cloned.1.call-done) | data formatting | bytes 10485760 | tf_op jit(solution)/shard_map/all_gather | solution.py:100
  156.3 10.1 %reshape.152 = bf16[1280,2048]{1,0:T(8,128)(2,1)} reshape(bf16[256,1,5,2048]{3,2,0,1:T(8,128)(2,1)} %copy.37) | data formatting | bytes 10485760 | tf_op jit(solution)/shard_map/reshape.6
  166.4 5.1 fusion.4
  171.6 3.3 fusion.2
  174.9 5.0 fusion
  179.9 9.8 %convert_element_type.145 = bf16[1,4,64,5,2048]{4,3,2,1,0:T(8,128)(2,1)} reshape(bf16[1,1280,2048]{2,1,0:T(8,128)(2,1)} %fusion) | data formatting | bytes 10485760 | tf_op jit(solution)/shard_map/convert_element_type | solution.py:113
  190.4 37.0 %all-gather.8.cloned.1.call-done = bf16[1024,2048]{1,0:T(8,128)(2,1)} async-done(((bf16[128,2048]{1,0:T(8,128)(2,1)}), bf16[1024,2048]{1,0:T(8,128)(2,1)}) %all-gather.8.cloned.1.call-update) | async-done | bytes 4194320 | tf_op jit(solution)/shard_map/all_gather | solution.py:126
  227.4 3.7 fusion.32
  232.6 3.3 add_convert_fusion.2
  235.9 74.4 %reduce-scatter.2.cloned.1.call-done = bf16[1,1,64,5,2048]{4,3,2,1,0:T(8,128)(2,1)} async-done(((bf16[1,4,64,5,2048]{4,3,2,1,0:T(8,128)(2,1)}), bf16[1,1,64,5,2048]{4,3,2,1,0:T(8,128)(2,1)}) %reduce-scatter.2.cloned.1.call-update) | async-done | bytes 1310736 | tf_op jit(solution)/shard_map/reduce_scatter | solution.py:112
  310.2 12.6 %all-to-all-start.1 = ((bf16[1,64,5,2048]{3,2,0,1:T(8,128)(2,1)}), bf16[1,64,5,2048]{3,2,0,1:T(8,128)(2,1)}, u32[]{:S(2)}, u32[]{:S(2)}) async-start(bf16[1,64,5,2048]{3,2,0,1:T(8,128)(2,1)} %bitcast.48), calls=%async_computation.2 | async-start | bytes 4194304 | tf_op jit(solution)/shard_map/all_to_all | solution.py:115
  322.9 49.1 %all-to-all-done.1 = bf16[1,64,5,2048]{3,2,0,1:T(8,128)(2,1)} async-done(((bf16[1,64,5,2048]{3,2,0,1:T(8,128)(2,1)}), bf16[1,64,5,2048]{3,2,0,1:T(8,128)(2,1)}, u32[]{:S(2)}, u32[]{:S(2)}) %all-to-all-start.1) | async-done | bytes 1310752 | tf_op jit(solution)/shard_map/all_to_all | solution.py:115
  379.7 3.8 reduce_sum.32
  383.5 18.9 %all-gather.6.cloned.1.call-done = bf16[1024,2048]{1,0:T(8,128)(2,1)} async-done(((bf16[128,2048]{1,0:T(8,128)(2,1)}), bf16[1024,2048]{1,0:T(8,128)(2,1)}) %all-gather.6.cloned.1.call-update) | async-done | bytes 4194320 | tf_op jit(solution)/shard_map/all_gather | solution.py:142
  402.4 190.3 %all-reduce.3.cloned.1.call-done = bf16[1024,2048]{1,0:T(8,128)(2,1)} async-done(((bf16[1024,2048]{1,0:T(8,128)(2,1)}), bf16[1024,2048]{1,0:T(8,128)(2,1)}) %all-reduce.3.cloned.1.call-update) | async-done | bytes 4194320 | tf_op jit(solution)/shard_map/psum | solution.py:140
  592.7 81.1 %all-gather.10.cloned.1.call-done = bf16[1024,2048]{1,0:T(8,128)(2,1)} async-done(((bf16[128,2048]{1,0:T(8,128)(2,1)}), bf16[1024,2048]{1,0:T(8,128)(2,1)}) %all-gather.10.cloned.1.call-update) | async-done | bytes 4194320 | tf_op jit(solution)/shard_map/all_gather | solution.py:143
  673.9 7.6 %add_convert_fusion.1 = bf16[1024,2048]{1,0:T(8,128)(2,1)S(1)} fusion(bf16[1024,2048]{1,0:T(8,128)(2,1)} %all-gather.10.cloned.1.call-done, bf16[1024,2048]{1,0:T(8,128)(2,1)} %all-reduce.3.cloned.1.call-done, bf16[1024,2048]{1,0:T(8,128)(2,1)} %all-gather.6.cloned.1.call-done), kind=kLoop, calls=%fused_computation.4 | loop fusion | flops 12582912 | bytes 16777216 | tf_op jit(solution)/shard_map/convert_element_type | solution.py:147
  (73 shorter events, 34.4 us)
Async XLA Ops:
  7.2 164.4 %copy-start = (bf16[1,2048,352]{1,2,0:T(8,128)(2,1)S(1)}, bf16[1,2048,352]{1,2,0:T(8,128)(2,1)}, u32[]{:S(2)}) copy-start(bf16[1,2048,352]{1,2,0:T(8,128)(2,1)} %param.21) | copy-start | bytes 4325380
  7.2 140.2 %all-gather.12.cloned.1.call-start = ((), (), s32[]{:S(2)}) async-start(), calls=%async_computation.8 | async-start | bytes 6553600 | tf_op jit(solution)/shard_map/all_gather | solution.py:100
  88.2 2.0 copy-start.3
  90.2 1.3 copy-start.6
  90.2 137.1 %all-gather.8.cloned.1.call-start = ((), (), s32[]{:S(2)}) async-start(), calls=%async_computation.4 | async-start | bytes 4718592 | tf_op jit(solution)/shard_map/all_gather | solution.py:126
  91.3 219.0 %reduce-scatter.2.cloned.1.call-start = ((), (), s32[]{:S(2)}) async-start(), calls=%async_computation.6 | async-start | bytes 10485760 | tf_op jit(solution)/shard_map/reduce_scatter | solution.py:112
  166.4 5.1 copy-start.2
  171.6 3.3 copy-start.5
  189.7 37.7 %copy-start.11 = (bf16[176,2048]{1,0:T(8,128)(2,1)S(1)}, bf16[176,2048]{1,0:T(8,128)(2,1)}, u32[]{:S(2)}) copy-start(bf16[176,2048]{1,0:T(8,128)(2,1)} %param.28) | copy-start | bytes 2162692
  189.7 212.7 %all-gather.6.cloned.1.call-start = ((), (), s32[]{:S(2)}) async-start(), calls=%async_computation.3 | async-start | bytes 4718592 | tf_op jit(solution)/shard_map/all_gather | solution.py:142
  190.3 40.8 %copy-start.4 = (bf16[1024,176]{0,1:T(8,128)(2,1)S(1)}, bf16[1024,176]{0,1:T(8,128)(2,1)}, u32[]{:S(2)}) copy-start(bf16[1024,176]{0,1:T(8,128)(2,1)} %param.24) | copy-start | bytes 1081348
  190.3 40.8 %copy-start.8 = (bf16[2048,176]{0,1:T(8,128)(2,1)S(1)}, bf16[2048,176]{0,1:T(8,128)(2,1)}, u32[]{:S(2)}) copy-start(bf16[2048,176]{0,1:T(8,128)(2,1)} %param.26) | copy-start | bytes 2162692
  190.3 40.8 %copy-start.9 = (bf16[1024,176]{0,1:T(8,128)(2,1)S(1)}, bf16[1024,176]{0,1:T(8,128)(2,1)}, u32[]{:S(2)}) copy-start(bf16[1024,176]{0,1:T(8,128)(2,1)} %param.25) | copy-start | bytes 1081348
  190.3 402.4 %all-reduce.3.cloned.1.call-start = ((), (), s32[]{:S(2)}) async-start(), calls=%async_computation.5 | async-start | bytes 8388608 | tf_op jit(solution)/shard_map/psum | solution.py:140
  231.1 1.4 copy-start.7
  310.2 61.7 %all-to-all-start.1 = ((bf16[1,64,5,2048]{3,2,0,1:T(8,128)(2,1)}), bf16[1,64,5,2048]{3,2,0,1:T(8,128)(2,1)}, u32[]{:S(2)}, u32[]{:S(2)}) async-start(bf16[1,64,5,2048]{3,2,0,1:T(8,128)(2,1)} %bitcast.48), calls=%async_computation.2 | async-start | bytes 4194304 | tf_op jit(solution)/shard_map/all_to_all | solution.py:115
  322.8 351.0 %all-gather.10.cloned.1.call-start = ((), (), s32[]{:S(2)}) async-start(), calls=%async_computation.7 | async-start | bytes 4718592 | tf_op jit(solution)/shard_map/all_gather | solution.py:143
  383.5 298.8 %copy-start.10 = (bf16[256,2048]{1,0:T(8,128)(2,1)S(1)}, bf16[256,2048]{1,0:T(8,128)(2,1)}, u32[]{:S(2)}) copy-start(bf16[256,2048]{1,0:T(8,128)(2,1)} %param.29) | copy-start | bytes 3145732
  682.3 2.1 copy-start.1
Sparse Core Ops, SparseCore 0:
  90.4 57.0 all-gather.11
  150.6 76.7 all-gather.7
  230.0 80.2 reduce-scatter.1
  312.7 89.6 all-gather.5
  404.9 187.7 all-reduce.2
  595.8 78.0 all-gather.9
where the time goes:
time: 693 us; the launch traced here: 691 us
  waiting for transfers between devices  490 us (71%)
  local copies, waits for them, and re-layouts  70.6 us (10%)
  blocking collectives  63.7 us (9%)
  matrix products  24 us (3%)
  other arithmetic  16.3 us (2%)
  between operations  14.4 us (2%)
  starting transfers between devices  12.8 us (2%)
    psum x1, waiting for transfers between devices, body(): lax.psum(partial_value.astype(jnp.bfloat16), 'tensor').astype(jnp.float32)  190 us
    all_gather x1, waiting for transfers between devices, body(): lax.all_gather(routed_total, 'tensor', axis=0, tiled=True)  81.1 us
    reduce_scatter x1, waiting for transfers between devices, body(): lax.psum_scatter(terms.astype(jnp.bfloat16), 'dp', scatter_dimension=1, t...  74.4 us
    all_to_all x1, blocking collectives, body(): lax.all_to_all(filled[:, None], ('expert', 'tensor'), split_axis=0, conca...  63.7 us
    all_to_all x1, waiting for transfers between devices, body(): lax.all_to_all(summed[:, 0].astype(jnp.bfloat16), ('expert', 'tensor'), s...  49.1 us
    all_gather x1, waiting for transfers between devices, body(): everyone = lax.all_gather(arrived[:, None], 'dp', axis=1, tiled=True)  38.2 us
    all_gather x1, waiting for transfers between devices, body(): group_shared = lax.all_gather(shared_grad, 'tensor', axis=0, tiled=True)  37 us
    all_gather x1, waiting for transfers between devices, body(): lax.all_gather(grad_out, 'tensor', axis=0, tiled=True)  18.9 us
  transfers between devices with their start and end apart: 7, of which 7 were waited for; matrix products, arithmetic and copies ran while one was open for 12% of the time, Pallas kernels for 0%

commit v1 on v0

--- a/solution.py
+++ b/solution.py
@@ -140,7 +140,10 @@
     shared_total = lax.psum(partial_value.astype(jnp.bfloat16), "tensor").astype(jnp.float32)
     group_grads, group_routed = (
         lax.all_gather(grad_out, "tensor", axis=0, tiled=True),
-        lax.all_gather(routed_total, "tensor", axis=0, tiled=True),
+        jnp.concatenate(
+            lax.all_to_all(jnp.stack([routed_total] * lax.axis_size("tensor")), "tensor", 0, 0),
+            axis=0,
+        ),
     )
     grad_group = (
         group_grads.astype(jnp.float32) + shared_total + group_routed.astype(jnp.float32)

time: 693 us -> 625 us (0.902)
  waiting for transfers between devices: 490 us -> 409 us
    all_gather x1 -> x0, waiting for transfers between devices: 81.1 us -> none  [body(): lax.all_gather(routed_total, 'tensor', axis=0, tiled=True)]
    all_gather x1, waiting for transfers between devices: 37 us -> 0.02 us  [body(): group_shared = lax.all_gather(shared_grad, 'tensor', axis=0, tiled=True)]
    reduce_scatter x1, waiting for transfers between devices: 74.4 us -> 108 us  [body(): lax.psum_scatter(terms.astype(jnp.bfloat16), 'dp', scatter_dimension=1, t...]
    psum x1, waiting for transfers between devices: 190 us -> 221 us  [body(): lax.psum(partial_value.astype(jnp.bfloat16), 'tensor').astype(jnp.float32)]
    all_gather x1, waiting for transfers between devices: 18.9 us -> 0.03 us  [body(): lax.all_gather(grad_out, 'tensor', axis=0, tiled=True)]
    all_to_all x1, waiting for transfers between devices: 49.1 us -> 40.4 us  [body(): lax.all_to_all(summed[:, 0].astype(jnp.bfloat16), ('expert', 'tensor'), s...]
  transfers between devices with their start and end apart: 7 -> 7, of which waited for: 7 -> 4; matrix products, arithmetic and copies ran while one was open for 12% -> 7% of each run, Pallas kernels for 0% -> 0%
where the time goes in v1:
time: 625 us; the launch traced here: 621 us
  waiting for transfers between devices  409 us (65%)
  local copies, waits for them, and re-layouts  73.9 us (12%)
  blocking collectives  63.7 us (10%)
  matrix products  24.1 us (4%)
  starting transfers between devices  18.6 us (3%)
  between operations  16 us (3%)
  other arithmetic  15.5 us (2%)
    psum x1, waiting for transfers between devices, body(): lax.psum(partial_value.astype(jnp.bfloat16), 'tensor').astype(jnp.float32)  221 us
    reduce_scatter x1, waiting for transfers between devices, body(): lax.psum_scatter(terms.astype(jnp.bfloat16), 'dp', scatter_dimension=1, t...  108 us
    all_to_all x1, blocking collectives, body(): lax.all_to_all(filled[:, None], ('expert', 'tensor'), split_axis=0, conca...  63.7 us
    all_to_all x1, waiting for transfers between devices, body(): lax.all_to_all(summed[:, 0].astype(jnp.bfloat16), ('expert', 'tensor'), s...  40.4 us
    all_gather x1, waiting for transfers between devices, body(): everyone = lax.all_gather(arrived[:, None], 'dp', axis=1, tiled=True)  39.2 us
    all_to_all x1, starting transfers between devices, body(): lax.all_to_all(summed[:, 0].astype(jnp.bfloat16), ('expert', 'tensor'), s...  12.7 us
  transfers between devices with their start and end apart: 7, of which 4 were waited for; matrix products, arithmetic and copies ran while one was open for 7% of the time, Pallas kernels for 0%

profile of v1, /device:TPU:1, one launch (start us, length us, event | category | flops | bytes accessed | tf_op | source)
XLA Modules:
  0.0 621.2 jit_solution(18179647012433842865)
XLA Ops:
  20.0 3.0 gather_fusion
  25.4 63.7 %all_to_all.23 = bf16[64,1,5,2048]{3,2,1,0:T(8,128)(2,1)S(1)} all-to-all(bf16[64,1,5,2048]{3,2,1,0:T(8,128)(2,1)S(1)} %bitcast.50), channel_id=1, replica_groups=mesh['dp'=4,'expert'=8,'tensor'=8] {'expert','tensor'}, dimensions={0} | all-to-all | bytes 2621440 | tf_op jit(solution)/shard_map/all_to_all | solution.py:97
  93.4 3.6 reshape.164
  98.9 3.5 copy.38
  102.3 3.9 reshape.163
  106.2 2.8 copy.39
  109.0 39.2 %all-gather.9.cloned.1.call-done = bf16[256,1,5,2048]{3,0,2,1:T(8,128)(2,1)} async-done(((bf16[64,1,5,2048]{3,0,2,1:T(8,128)(2,1)}), bf16[256,1,5,2048]{3,0,2,1:T(8,128)(2,1)}) %all-gather.9.cloned.1.call-update) | async-done | bytes 5242896 | tf_op jit(solution)/shard_map/all_gather | solution.py:100
  148.2 8.9 %copy.37 = bf16[256,1,5,2048]{3,2,0,1:T(8,128)(2,1)} copy(bf16[256,1,5,2048]{3,0,2,1:T(8,128)(2,1)} %all-gather.9.cloned.1.call-done) | data formatting | bytes 10485760 | tf_op jit(solution)/shard_map/all_gather | solution.py:100
  157.1 10.0 %reshape.157 = bf16[1280,2048]{1,0:T(8,128)(2,1)} reshape(bf16[256,1,5,2048]{3,2,0,1:T(8,128)(2,1)} %copy.37) | data formatting | bytes 10485760 | tf_op jit(solution)/shard_map/reshape.6
  167.2 5.1 fusion.5
  172.3 3.3 fusion.3
  175.6 5.0 fusion.1
  180.6 9.8 %convert_element_type.150 = bf16[1,4,64,5,2048]{4,3,2,1,0:T(8,128)(2,1)} reshape(bf16[1,1280,2048]{2,1,0:T(8,128)(2,1)} %fusion.1) | data formatting | bytes 10485760 | tf_op jit(solution)/shard_map/convert_element_type | solution.py:113
  193.0 108.0 %reduce-scatter.2.cloned.1.call-done = bf16[1,1,64,5,2048]{4,3,2,1,0:T(8,128)(2,1)} async-done(((bf16[1,4,64,5,2048]{4,3,2,1,0:T(8,128)(2,1)}), bf16[1,1,64,5,2048]{4,3,2,1,0:T(8,128)(2,1)}) %reduce-scatter.2.cloned.1.call-update) | async-done | bytes 1310736 | tf_op jit(solution)/shard_map/reduce_scatter | solution.py:112
  301.1 12.7 %all-to-all-start.1 = ((bf16[1,64,5,2048]{3,2,0,1:T(8,128)(2,1)}), bf16[1,64,5,2048]{3,2,0,1:T(8,128)(2,1)}, u32[]{:S(2)}, u32[]{:S(2)}) async-start(bf16[1,64,5,2048]{3,2,0,1:T(8,128)(2,1)} %bitcast.51), calls=%async_computation.2 | async-start | bytes 4194304 | tf_op jit(solution)/shard_map/all_to_all | solution.py:115
  313.9 3.8 fusion.33
  319.2 3.3 add_convert_fusion.1
  322.5 40.4 %all-to-all-done.1 = bf16[1,64,5,2048]{3,2,0,1:T(8,128)(2,1)} async-done(((bf16[1,64,5,2048]{3,2,0,1:T(8,128)(2,1)}), bf16[1,64,5,2048]{3,2,0,1:T(8,128)(2,1)}, u32[]{:S(2)}, u32[]{:S(2)}) %all-to-all-start.1) | async-done | bytes 1310752 | tf_op jit(solution)/shard_map/all_to_all | solution.py:115
  362.9 2.5 reshape.165
  365.4 2.7 gather_fusion.1
  370.6 3.0 reduce_sum.32
  376.1 5.7 all-to-all-start.2
  381.9 221.2 %all-reduce.3.cloned.1.call-done = bf16[1024,2048]{1,0:T(8,128)(2,1)} async-done(((bf16[1024,2048]{1,0:T(8,128)(2,1)}), bf16[1024,2048]{1,0:T(8,128)(2,1)}) %all-reduce.3.cloned.1.call-update) | async-done | bytes 4194320 | tf_op jit(solution)/shard_map/psum | solution.py:140
  603.1 7.6 %fusion = bf16[1024,2048]{1,0:T(8,128)(2,1)S(1)} fusion(bf16[1024,2048]{1,0:T(8,128)(2,1)} %all-reduce.3.cloned.1.call-done, bf16[1024,2048]{1,0:T(8,128)(2,1)} %all-gather.5.cloned.1.call-done, bf16[8,128,2048]{2,1,0:T(8,128)(2,1)} %all-to-all-done.2), kind=kLoop, calls=%fused_computation.5 | loop fusion | flops 12582912 | bytes 16777216 | tf_op jit(solution)/shard_map/convert_element_type | solution.py:150
  (73 shorter events, 32.5 us)
Async XLA Ops:
  8.0 164.3 %copy-start = (bf16[1,2048,352]{1,2,0:T(8,128)(2,1)S(1)}, bf16[1,2048,352]{1,2,0:T(8,128)(2,1)}, u32[]{:S(2)}) copy-start(bf16[1,2048,352]{1,2,0:T(8,128)(2,1)} %param.21) | copy-start | bytes 4325380
  8.0 140.2 %all-gather.9.cloned.1.call-start = ((), (), s32[]{:S(2)}) async-start(), calls=%async_computation.8 | async-start | bytes 6553600 | tf_op jit(solution)/shard_map/all_gather | solution.py:100
  89.1 2.0 copy-start.6
  91.1 210.0 %reduce-scatter.2.cloned.1.call-start = ((), (), s32[]{:S(2)}) async-start(), calls=%async_computation.7 | async-start | bytes 10485760 | tf_op jit(solution)/shard_map/reduce_scatter | solution.py:112
  167.2 5.1 copy-start.2
  172.3 3.3 copy-start.5
  190.4 1.0 copy-start.3
  190.4 123.4 %all-gather.7.cloned.1.call-start = ((), (), s32[]{:S(2)}) async-start(), calls=%async_computation.5 | async-start | bytes 4718592 | tf_op jit(solution)/shard_map/all_gather | solution.py:126
  192.4 189.4 %all-gather.5.cloned.1.call-start = ((), (), s32[]{:S(2)}) async-start(), calls=%async_computation.4 | async-start | bytes 4718592 | tf_op jit(solution)/shard_map/all_gather | solution.py:142
  301.1 12.8 %copy-start.11 = (bf16[176,2048]{1,0:T(8,128)(2,1)S(1)}, bf16[176,2048]{1,0:T(8,128)(2,1)}, u32[]{:S(2)}) copy-start(bf16[176,2048]{1,0:T(8,128)(2,1)} %param.28) | copy-start | bytes 2162692
  301.1 61.8 %all-to-all-start.1 = ((bf16[1,64,5,2048]{3,2,0,1:T(8,128)(2,1)}), bf16[1,64,5,2048]{3,2,0,1:T(8,128)(2,1)}, u32[]{:S(2)}, u32[]{:S(2)}) async-start(bf16[1,64,5,2048]{3,2,0,1:T(8,128)(2,1)} %bitcast.51), calls=%async_computation.2 | async-start | bytes 4194304 | tf_op jit(solution)/shard_map/all_to_all | solution.py:115
  313.8 4.0 copy-start.4
  313.8 3.9 copy-start.8
  313.8 3.9 copy-start.9
  313.8 289.3 %all-reduce.3.cloned.1.call-start = ((), (), s32[]{:S(2)}) async-start(), calls=%async_computation.6 | async-start | bytes 8388608 | tf_op jit(solution)/shard_map/psum | solution.py:140
  317.7 1.4 copy-start.7
  376.1 227.0 %all-to-all-start.2 = ((bf16[8,128,2048]{2,1,0:T(8,128)(2,1)}), bf16[8,128,2048]{2,1,0:T(8,128)(2,1)}, u32[]{:S(2)}, u32[]{:S(2)}) async-start(bf16[8,128,2048]{2,1,0:T(8,128)(2,1)} %stack.2), calls=%async_computation.3 | async-start | bytes 8388608 | tf_op jit(solution)/shard_map/all_to_all | solution.py:144
  381.8 229.7 %copy-start.10 = (bf16[256,2048]{1,0:T(8,128)(2,1)S(1)}, bf16[256,2048]{1,0:T(8,128)(2,1)}, u32[]{:S(2)}) copy-start(bf16[256,2048]{1,0:T(8,128)(2,1)} %param.29) | copy-start | bytes 3145732
  611.6 2.1 copy-start.1
Sparse Core Ops, SparseCore 0:
  91.2 57.0 all-gather.8
  190.6 110.4 reduce-scatter.1
Sparse Core Ops, SparseCore 1:
  194.1 92.3 all-gather.6
  289.0 90.4 all-gather.4
  381.9 221.1 all-reduce.2
